TPU v7x, 32 devices: a whole 2x2x4 slice. The times are simulated.
32 devices in a mesh: groups: 2 (over y), img: 4 (over z), head: 4 (over x, core).
Axes of the slice: x: 2, y: 2, z: 4, core: 2. Of those that a mesh axis runs over, the one named last changes fastest.
Arguments:
- descriptors: bfloat16 [32, 384, 256], P(('groups', 'img')), parts along dimension 0, may hold values from -22 to 22
- pair_slots: int32 [16, 2], P(('groups', 'img')), parts along dimension 0, may hold values from -1 to 15, as said below
- valid_counts: int32 [32], P('groups'), parts along dimension 0, may hold values from 96 to 384, as said below
- shared_proj: bfloat16 [256, 256], P(None, 'head'), may hold values from -0.375 to 0.375
- value_proj: bfloat16 [256, 256], P(None, 'head'), may hold values from -0.375 to 0.375
- merge_proj: bfloat16 [256, 256], P('head'), may hold values from -0.375 to 0.375
- first_layer: bfloat16 [512, 512], replicated, may hold values from -0.25 to 0.25
- second_layer: bfloat16 [512, 256], replicated, may hold values from -0.25 to 0.25
- norm_gain: float32 [512], replicated, may hold values from 0.25 to 1.75
- norm_bias: float32 [512], replicated, may hold values from -3 to 3
- second_bias: float32 [256], replicated, may hold values from -3 to 3
Outputs:
- updated: bfloat16 [12288, 256], P(('groups', 'img', 'head')), parts along dimension 0
There are 2 independent parts, one for each index of `groups`. A program takes and returns all parts, laid end to end along the dimension named above; an argument that names none is the same for every part. Nothing has to cross between parts.
Inputs may be any that keep to these rules, and one draw needn't show every extreme that they name: `pair_slots`: rows are in blocks of 2, block k being the pairs of owner k; in each block the non-empty slots come first and an empty slot is -1 in both columns; some block is full in every draw; the images named in one block lie in distinct blocks of 4 consecutive images. `valid_counts`: some image has all 384 keypoints valid.
All inputs are finite; a program needn't handle non-finite values.
Results may differ from a plain program's by a relative error of at most 0.0052.
Values may be sent and summed in bfloat16 or wider, within the bound.
A program may use at most 64 MiB of HBM per device.

v0:
```python
import math

import jax
import jax.numpy as jnp
from jax import lax
from jax.sharding import PartitionSpec as P

HD = 64


def masked_softmax(scores, allowed, axis_index):
    filled = jnp.where(allowed, scores, -jnp.inf)
    largest = jnp.max(filled, axis=axis_index, keepdims=True)
    powers = jnp.exp(filled - largest)
    return powers / jnp.sum(powers, axis=axis_index, keepdims=True)


def on_device(
    descriptors,
    pair_slots,
    valid_counts,
    shared_proj,
    value_proj,
    merge_proj,
    first_layer,
    second_layer,
    norm_gain,
    norm_bias,
    second_bias,
):
    img_count = lax.axis_size("img")
    owner_index = lax.axis_index("img")
    head_count = lax.axis_size("head")
    head_index = lax.axis_index("head")
    per_device, points, width = descriptors.shape
    capacity = pair_slots.shape[0]
    lanes = value_proj.shape[1]
    heads_here = lanes // HD
    flat_rows = descriptors.reshape(per_device * points, width)
    both_proj = jnp.concatenate([shared_proj, value_proj], axis=1)
    all_slots = lax.all_gather(pair_slots, "img", axis=0, tiled=True)
    slot_owner = jnp.arange(all_slots.shape[0], dtype=jnp.int32) // capacity
    owner_hot = (slot_owner[:, None] == jnp.arange(img_count, dtype=jnp.int32)[None, :]).astype(
        jnp.float32
    )
    local_ids = owner_index * per_device + jnp.arange(per_device, dtype=jnp.int32)
    touches = (
        (all_slots[:, 0:1] == local_ids[None, :]) | (all_slots[:, 1:2] == local_ids[None, :])
    ).astype(jnp.float32)
    needed = jnp.dot(owner_hot.T, touches) > 0.5
    needed_mask = needed.astype(jnp.bfloat16)
    local_pack = (
        jnp.dot(flat_rows, both_proj, preferred_element_type=jnp.float32)
        .astype(jnp.bfloat16)
        .reshape(per_device, points, 2 * lanes)
    )
    outgoing = jnp.einsum(
        "jt,tkc->jkc", needed_mask, local_pack, preferred_element_type=jnp.bfloat16
    )
    incoming = lax.all_to_all(outgoing, "img", split_axis=0, concat_axis=0, tiled=True)
    positions = jnp.arange(points, dtype=jnp.int32)
    scale = 1.0 / math.sqrt(HD)
    firsts = pair_slots[:, 0]
    seconds = pair_slots[:, 1]
    live = firsts >= 0

    def one_pair(slot, replies):
        first_img = jnp.maximum(firsts[slot], 0)
        second_img = jnp.maximum(seconds[slot], 0)
        first_src = first_img // per_device
        second_src = second_img // per_device
        first_pack = lax.dynamic_index_in_dim(incoming, first_src, 0, keepdims=False)
        second_pack = lax.dynamic_index_in_dim(incoming, second_src, 0, keepdims=False)
        first_keys = first_pack[:, :lanes].reshape(points, heads_here, HD)
        first_vals = first_pack[:, lanes:].reshape(points, heads_here, HD)
        second_keys = second_pack[:, :lanes].reshape(points, heads_here, HD)
        second_vals = second_pack[:, lanes:].reshape(points, heads_here, HD)
        scores = (
            jnp.einsum("ihd,jhd->hij", first_keys, second_keys, preferred_element_type=jnp.float32)
            * scale
        )
        row_weights = masked_softmax(
            scores, (positions < valid_counts[second_img])[None, None, :], 2
        ).astype(jnp.bfloat16)
        col_weights = masked_softmax(
            scores, (positions < valid_counts[first_img])[None, :, None], 1
        ).astype(jnp.bfloat16)
        to_first = (
            jnp.einsum("hij,jhd->ihd", row_weights, second_vals, preferred_element_type=jnp.float32)
            .astype(jnp.bfloat16)
            .reshape(points, lanes)
        )
        to_second = (
            jnp.einsum("hij,ihd->jhd", col_weights, first_vals, preferred_element_type=jnp.float32)
            .astype(jnp.bfloat16)
            .reshape(points, lanes)
        )
        keep = live[slot]
        old_first = lax.dynamic_index_in_dim(replies, first_src, 0, keepdims=False)
        replies = lax.dynamic_update_index_in_dim(
            replies, jnp.where(keep, to_first, old_first), first_src, 0
        )
        old_second = lax.dynamic_index_in_dim(replies, second_src, 0, keepdims=False)
        replies = lax.dynamic_update_index_in_dim(
            replies, jnp.where(keep, to_second, old_second), second_src, 0
        )
        return replies

    empty = jnp.zeros((img_count, points, lanes), jnp.bfloat16)
    replies = lax.fori_loop(0, capacity, one_pair, empty)
    returned = lax.all_to_all(replies, "img", split_axis=0, concat_axis=0, tiled=True)
    messages = jnp.einsum(
        "jt,jkc->tkc", needed_mask, returned, preferred_element_type=jnp.float32
    ).astype(jnp.bfloat16)
    message_rows = messages.reshape(per_device * points, lanes)
    share = per_device * points // head_count
    projected = lax.psum_scatter(
        jnp.dot(message_rows, merge_proj, preferred_element_type=jnp.float32),
        "head",
        scatter_dimension=0,
        tiled=True,
    )
    own_rows = lax.dynamic_slice_in_dim(flat_rows, head_index * share, share, 0)
    joined = jnp.concatenate([own_rows, projected.astype(jnp.bfloat16)], axis=1)
    hidden = jnp.dot(joined, first_layer, preferred_element_type=jnp.float32)
    center = jnp.mean(hidden, axis=1, keepdims=True)
    spread = jnp.mean(jnp.square(hidden - center), axis=1, keepdims=True)
    normed = (hidden - center) * lax.rsqrt(spread + 1e-05) * norm_gain + norm_bias
    active = jax.nn.gelu(normed, approximate=False).astype(jnp.bfloat16)
    update = jnp.dot(active, second_layer, preferred_element_type=jnp.float32) + second_bias
    return (own_rows.astype(jnp.float32) + update).astype(jnp.bfloat16)


def solution(mesh):
    return jax.shard_map(
        on_device,
        mesh=mesh,
        in_specs=(
            P(("groups", "img"), None, None),
            P(("groups", "img"), None),
            P("groups"),
            P(None, "head"),
            P(None, "head"),
            P("head", None),
            P(),
            P(),
            P(),
            P(),
            P(),
        ),
        out_specs=P(("groups", "img", "head"), None),
        check_vma=False,
    )
```

profile of v0, /device:TPU:0, one launch (start us, length us, event | category | flops | bytes accessed | tf_op | source)
XLA Modules:
  0.0 102.3 jit_solution(13850741200174262226)
XLA Ops:
  6.5 13.0 %all-gather = s32[4,2,2]{2,1,0:T(2,128)S(1)} all-gather(s32[1,2,2]{2,1,0:T(2,128)} %bitcast.74), channel_id=1, replica_groups=mesh['groups'=2,'img'=4,'head'=4] {'img'}, dimensions={0}, use_global_device_ids=true | all-gather | bytes 80 | tf_op jit(solution)/shard_map/all_gather | solution.py:41
  19.7 1.2 %fusion.18 = bf16[1536,128]{0,1:T(8,128)(2,1)S(1)} fusion(bf16[1536,256]{1,0:T(8,128)(2,1)S(1)} %bitcast.70, bf16[256,64]{0,1:T(8,128)(2,1)} %param.17, bf16[256,64]{0,1:T(8,128)(2,1)} %param.16), kind=kOutput, calls=%fused_computation.31 | convolution fusion | flops 100990976 | bytes 1245184 | tf_op jit(solution)/shard_map/dot_general | solution.py:53
  21.0 0.3 copy.24
  21.6 0.4 fusion.117
  22.0 0.8 copy.25
  22.8 3.5 %all-to-all-start = ((bf16[4,384,128]{2,1,0:T(8,128)(2,1)}), bf16[4,384,128]{2,1,0:T(8,128)(2,1)S(1)}, u32[]{:S(2)}, u32[]{:S(2)}) async-start(bf16[4,384,128]{2,1,0:T(8,128)(2,1)} %copy.25), calls=%async_computation | async-start | bytes 786432 | tf_op jit(solution)/shard_map/all_to_all | solution.py:60
  26.5 9.7 %all-to-all-done = bf16[4,384,128]{2,1,0:T(8,128)(2,1)S(1)} async-done(((bf16[4,384,128]{2,1,0:T(8,128)(2,1)}), bf16[4,384,128]{2,1,0:T(8,128)(2,1)S(1)}, u32[]{:S(2)}, u32[]{:S(2)}) %all-to-all-start) | async-done | bytes 393248 | tf_op jit(solution)/shard_map/all_to_all | solution.py:60
  36.2 16.2 %while.18 = (s32[]{:T(128)}, bf16[4,384,64]{1,2,0:T(8,128)(2,1)S(1)}, pred[2]{0:T(512)(128)(4,1)S(1)}, s32[2]{0:T(128)S(1)}, bf16[4,384,128]{2,1,0:T(8,128)(2,1)...) while((s32[]{:T(128)}, ...), condition=%wide.region_5.6_spmd.clone.clone, body=%wide.region_0.5_spmd.clone.clone.sunk | while | flops 59522328 | bytes 3363533 | solution.py:110
  36.2 0.7 dynamic_slice.144
  37.5 0.6 dynamic_slice.143
  38.8 0.7 fusion.135
  39.5 1.3 %iota_compare_fusion.5 = (pred[384]{0:T(512)(128)(4,1)S(1)}, pred[384]{0:T(512)(128)(4,1)S(1)}) fusion(s32[]{:T(128)} %bitcast.66, s32[]{:T(128)} %bitcast.67), kind=kLoop, calls=%fused_computation.26.clone.1 | loop fusion | flops 768 | bytes 776 | tf_op jit(solution)/shard_map/while/body/eval_jaxpr/lt | solution.py:86
  40.8 0.4 select_reduce_fusion.3
  41.1 0.4 fusion.136
  41.5 0.7 dynamic_slice.145
  42.2 1.1 %fusion.137 = bf16[4,384,64]{1,2,0:T(8,128)(2,1)S(1)} fusion(bf16[4,384,64]{1,2,0:T(8,128)(2,1)S(1)} %get-tuple-element.386, s32[]{:T(128)S(6)} %select_n.204, f32[384,384]{1,0:T(8,128)S(1)} %get-tuple-element.366, f32[384]{0:T(512)S(1)} %get-tuple-element.369, f32[384]{0:T(512)S(1)} %get-tuple-element.368, ...), kind=kOutput, calls=%fused_computation.9.clone.1 | convolution fusion | flops 19513344 | bytes 791045 | tf_op jit(solution)/shard_map/while/body/eval_jaxpr/hij,jhd->ihd/dot_general | solution.py:89
  43.3 1.0 %fusion.138 = bf16[4,384,64]{1,2,0:T(8,128)(2,1)S(1)} fusion(bf16[4,384,64]{1,2,0:T(8,128)(2,1)S(1)} %fusion.137, s32[]{:T(128)S(6)} %select_n.206, f32[384,384]{1,0:T(8,128)S(1)} %get-tuple-element.366, f32[384]{0:T(512)S(1)} %get-tuple-element.370, f32[384]{0:T(512)S(1)} %get-tuple-element.367, pred[384]{0:T(512)(128)(4,1)S(1)} %get-tuple-element.362, ...), kind=kOutput, calls=%fused_computation.7.clone.1 | convolution fusion | flops 19513344 | bytes 791045 | tf_op jit(solution)/shard_map/while/body/eval_jaxpr/hij,ihd->jhd/dot_general | solution.py:94
  44.3 0.7 dynamic_slice.144
  45.6 0.6 dynamic_slice.143
  46.9 0.7 fusion.135
  47.6 1.3 %iota_compare_fusion.5 = (pred[384]{0:T(512)(128)(4,1)S(1)}, pred[384]{0:T(512)(128)(4,1)S(1)}) fusion(s32[]{:T(128)} %bitcast.66, s32[]{:T(128)} %bitcast.67), kind=kLoop, calls=%fused_computation.26.clone.1 | loop fusion | flops 768 | bytes 776 | tf_op jit(solution)/shard_map/while/body/eval_jaxpr/lt | solution.py:86
  48.9 0.4 select_reduce_fusion.3
  49.2 0.4 fusion.136
  49.6 0.7 dynamic_slice.145
  50.3 1.1 %fusion.137 = bf16[4,384,64]{1,2,0:T(8,128)(2,1)S(1)} fusion(bf16[4,384,64]{1,2,0:T(8,128)(2,1)S(1)} %get-tuple-element.386, s32[]{:T(128)S(6)} %select_n.204, f32[384,384]{1,0:T(8,128)S(1)} %get-tuple-element.366, f32[384]{0:T(512)S(1)} %get-tuple-element.369, f32[384]{0:T(512)S(1)} %get-tuple-element.368, ...), kind=kOutput, calls=%fused_computation.9.clone.1 | convolution fusion | flops 19513344 | bytes 791045 | tf_op jit(solution)/shard_map/while/body/eval_jaxpr/hij,jhd->ihd/dot_general | solution.py:89
  51.4 1.0 %fusion.138 = bf16[4,384,64]{1,2,0:T(8,128)(2,1)S(1)} fusion(bf16[4,384,64]{1,2,0:T(8,128)(2,1)S(1)} %fusion.137, s32[]{:T(128)S(6)} %select_n.206, f32[384,384]{1,0:T(8,128)S(1)} %get-tuple-element.366, f32[384]{0:T(512)S(1)} %get-tuple-element.370, f32[384]{0:T(512)S(1)} %get-tuple-element.367, pred[384]{0:T(512)(128)(4,1)S(1)} %get-tuple-element.362, ...), kind=kOutput, calls=%fused_computation.7.clone.1 | convolution fusion | flops 19513344 | bytes 791045 | tf_op jit(solution)/shard_map/while/body/eval_jaxpr/hij,ihd->jhd/dot_general | solution.py:94
  52.4 9.3 %all_to_all.10 = bf16[4,384,64]{1,2,0:T(8,128)(2,1)S(1)} all-to-all(bf16[4,384,64]{1,2,0:T(8,128)(2,1)S(1)} %get-tuple-element.231), channel_id=1, replica_groups=mesh['groups'=2,'img'=4,'head'=4] {'img'}, dimensions={0} | all-to-all | bytes 393216 | tf_op jit(solution)/shard_map/all_to_all | solution.py:111
  62.1 1.6 %fusion.118 = f32[1536,256]{1,0:T(8,128)} fusion(bf16[1536,64]{0,1:T(8,128)(2,1)S(1)} %bitcast.71, bf16[64,256]{1,0:T(8,128)(2,1)S(1)} %copy-done.3), kind=kOutput, calls=%fused_computation.156 | convolution fusion | flops 50331648 | bytes 1802240 | tf_op jit(solution)/shard_map/dot_general | solution.py:118
  63.8 27.1 %reduce-scatter.2.cloned.1.call-done = f32[384,256]{1,0:T(8,128)} async-done(((f32[1536,256]{1,0:T(8,128)}), f32[384,256]{1,0:T(8,128)}) %reduce-scatter.2.cloned.1.call-update) | async-done | bytes 393232 | tf_op jit(solution)/shard_map/reduce_scatter | solution.py:117
  90.9 1.0 convert_element_type.86
  91.9 0.5 fusion.116
  92.6 2.8 %fusion.20 = bf16[384,256]{1,0:T(8,128)(2,1)} fusion(bf16[512,256]{1,0:T(8,128)(2,1)S(1)} %copy-done.5, f32[384,512]{1,0:T(8,128)S(1)} %get-tuple-element.305, f32[512]{0:T(512)S(1)} %copy-done.6, f32[512]{0:T(512)S(1)} %copy-done.7, f32[384]{0:T(512)S(1)} %add_rsqrt_fusion, f32[384]{0:T(512)S(1)} %broadcast_multiply_fusion, ...), kind=kOutput, calls=%fused_computation.35 | convolution fusion | flops 114622464 | bytes 1449984 | tf_op jit(solution)/shard_map/dot_general | solution.py:130
  (38 shorter events, 1.6 us)
Async XLA Ops:
  6.5 13.2 %copy-start = (bf16[4,384,256]{2,1,0:T(8,128)(2,1)S(1)}, bf16[4,384,256]{2,1,0:T(8,128)(2,1)}, u32[]{:S(2)}) copy-start(bf16[4,384,256]{2,1,0:T(8,128)(2,1)} %param.13) | copy-start | bytes 2359300
  21.0 5.3 %copy-start.4 = (s32[2,2]{1,0:T(2,128)S(1)}, s32[2,2]{1,0:T(2,128)}, u32[]{:S(2)}) copy-start(s32[2,2]{1,0:T(2,128)} %param.14) | copy-start | bytes 52
  21.4 14.8 %copy-start.2 = (s32[16]{0:T(128)S(1)}, s32[16]{0:T(128)}, u32[]{:S(2)}) copy-start(s32[16]{0:T(128)} %param.15) | copy-start | bytes 196
  22.8 13.4 %all-to-all-start = ((bf16[4,384,128]{2,1,0:T(8,128)(2,1)}), bf16[4,384,128]{2,1,0:T(8,128)(2,1)S(1)}, u32[]{:S(2)}, u32[]{:S(2)}) async-start(bf16[4,384,128]{2,1,0:T(8,128)(2,1)} %copy.25), calls=%async_computation | async-start | bytes 786432 | tf_op jit(solution)/shard_map/all_to_all | solution.py:60
  26.2 64.6 %reduce-scatter.2.cloned.1.call-start = ((), (), s32[]{:S(2)}) async-start(), calls=%async_computation.3 | async-start | bytes 1966080 | tf_op jit(solution)/shard_map/reduce_scatter | solution.py:117
  36.2 25.9 %copy-start.3 = (bf16[64,256]{1,0:T(8,128)(2,1)S(1)}, bf16[64,256]{1,0:T(8,128)(2,1)}, u32[]{:S(2)}) copy-start(bf16[64,256]{1,0:T(8,128)(2,1)} %param.18) | copy-start | bytes 98308
  63.6 28.2 %copy-start.1 = (bf16[512,512]{1,0:T(8,128)(2,1)S(1)}, bf16[512,512]{1,0:T(8,128)(2,1)}, u32[]{:S(2)}) copy-start(bf16[512,512]{1,0:T(8,128)(2,1)} %param.19) | copy-start | bytes 1572868
  63.7 28.9 %copy-start.5 = (bf16[512,256]{1,0:T(8,128)(2,1)S(1)}, bf16[512,256]{1,0:T(8,128)(2,1)}, u32[]{:S(2)}) copy-start(bf16[512,256]{1,0:T(8,128)(2,1)} %param.20) | copy-start | bytes 786436
  63.7 28.9 %copy-start.6 = (f32[512]{0:T(512)S(1)}, f32[512]{0:T(512)}, u32[]{:S(2)}) copy-start(f32[512]{0:T(512)} %param.22) | copy-start | bytes 6148
  63.7 28.9 %copy-start.7 = (f32[512]{0:T(512)S(1)}, f32[512]{0:T(512)}, u32[]{:S(2)}) copy-start(f32[512]{0:T(512)} %param.21) | copy-start | bytes 6148
  63.7 28.9 %copy-start.8 = (f32[256]{0:T(256)S(1)}, f32[256]{0:T(256)}, u32[]{:S(2)}) copy-start(f32[256]{0:T(256)} %param.23) | copy-start | bytes 3076
Sparse Core Ops, SparseCore 0:
  63.8 27.0 reduce-scatter.1
where the time goes:
time: 103 us; the launch traced here: 102 us
  waiting for transfers between devices  36.8 us (36%)
  blocking collectives  22.3 us (22%)
  between operations  13.6 us (13%)
  matrix products  11.8 us (11%)
  local copies, waits for them, and re-layouts  6.99 us (7%)
  other arithmetic  4.53 us (4%)
  starting transfers between devices  3.5 us (3%)
  loops' own time  2.71 us (3%)
    reduce_scatter x1, waiting for transfers between devices, on_device(): lax.psum_scatter(jnp.dot(message_rows, merge_proj, preferred_element_type...  27.1 us
    all_gather x1, blocking collectives, on_device(): all_slots = lax.all_gather(pair_slots, 'img', axis=0, tiled=True)  13 us
    all_to_all x1, waiting for transfers between devices, on_device(): lax.all_to_all(outgoing, 'img', split_axis=0, concat_axis=0, tiled=True)  9.66 us
    all_to_all x1, blocking collectives, on_device(): lax.all_to_all(replies, 'img', split_axis=0, concat_axis=0, tiled=True)  9.32 us
    all_to_all x1, starting transfers between devices, on_device(): lax.all_to_all(outgoing, 'img', split_axis=0, concat_axis=0, tiled=True)  3.46 us
    dot_general x1, matrix products, on_device(): jnp.dot(active, second_layer, preferred_element_type=jnp.float32)  2.77 us
    another operation x1, loops' own time, on_device(): replies = lax.fori_loop(0, capacity, one_pair, empty)  2.71 us
    lt x2, other arithmetic, one_pair(): positions < valid_counts[first_img]  2.5 us
  transfers between devices with their start and end apart: 2, of which 2 were waited for; matrix products, arithmetic and copies ran while one was open for 0% of the time, Pallas kernels for 0%

commit v1 on v0

v1 whole, which is shorter than its diff:
```python
import functools
import math

import jax
import jax.numpy as jnp
from jax import lax
from jax.experimental import pallas as pl
from jax.experimental.pallas import tpu as pltpu
from jax.sharding import PartitionSpec as P

HD = 64
MESH = pl.DeviceIdType.MESH
FAR = -1e30


def each(count, body):
    if count <= 8:
        for step in range(count):
            body(step)
    else:
        lax.fori_loop(0, count, lambda step, carry: (body(step), carry)[1], 0)


def fold(count, body, start):
    if count <= 8:
        for step in range(count):
            start = body(step, start)
        return start
    return lax.fori_loop(0, count, body, start)


def kernel(
    owners,
    heads,
    slots,
    counts,
    desc_in,
    shared_in,
    value_in,
    merge_in,
    first_in,
    second_in,
    gain_in,
    bias_in,
    last_in,
    out,
    desc,
    shared,
    value,
    merge_all,
    first,
    second,
    gain,
    bias,
    last,
    all_slots,
    pack,
    outgoing,
    incoming,
    replies,
    returned,
    sent,
    got,
    base,
    merge_top,
    local_sem,
    slot_send,
    slot_recv,
    merge_send,
    merge_recv,
    pack_send,
    pack_recv,
    reply_send,
    reply_recv,
    sent_send,
    sent_recv,
):
    per, points, width = desc.shape
    half = points // 2
    capacity = slots.shape[0]
    me = lax.axis_index("img")
    here = lax.axis_index("head")

    def owner_at(shift):
        return lax.rem(me + shift, owners)

    def head_at(shift):
        return lax.rem(here + shift, heads)

    pairs = [
        (desc_in, desc),
        (shared_in, shared),
        (value_in, value),
        (merge_in, merge_all.at[here]),
        (first_in, first),
        (second_in, second),
        (gain_in, gain),
        (bias_in, bias),
        (last_in, last),
    ]
    local = [
        pltpu.make_async_copy(src, dst, local_sem.at[at]) for at, (src, dst) in enumerate(pairs)
    ]
    for copy in local:
        copy.start()

    def keep_slots(slot):
        all_slots[me, 0, slot * 2] = slots[slot, 0]
        all_slots[me, 0, slot * 2 + 1] = slots[slot, 1]

    each(capacity, keep_slots)

    barrier = pltpu.get_barrier_semaphore()
    each(
        owners - 1,
        lambda step: pl.semaphore_signal(
            barrier, inc=1, device_id={"img": owner_at(step + 1)}, device_id_type=MESH
        ),
    )
    for step in range(1, heads):
        pl.semaphore_signal(
            barrier, inc=1, device_id={"head": head_at(step)}, device_id_type=MESH
        )
    pl.semaphore_wait(barrier, owners + heads - 2)

    def slot_copy(step):
        return pltpu.make_async_remote_copy(
            src_ref=all_slots.at[me],
            dst_ref=all_slots.at[me],
            send_sem=slot_send.at[step],
            recv_sem=slot_recv.at[step],
            device_id={"img": owner_at(step)},
            device_id_type=MESH,
        )

    def merge_copy(step):
        return pltpu.make_async_remote_copy(
            src_ref=merge_in,
            dst_ref=merge_all.at[here],
            send_sem=merge_send.at[step],
            recv_sem=merge_recv.at[step],
            device_id={"head": head_at(step)},
            device_id_type=MESH,
        )

    def pack_copy(step):
        return pltpu.make_async_remote_copy(
            src_ref=outgoing.at[step],
            dst_ref=incoming.at[me],
            send_sem=pack_send.at[step],
            recv_sem=pack_recv.at[step],
            device_id={"img": owner_at(step)},
            device_id_type=MESH,
        )

    def reply_copy(step):
        return pltpu.make_async_remote_copy(
            src_ref=replies.at[step],
            dst_ref=returned.at[me],
            send_sem=reply_send.at[step],
            recv_sem=reply_recv.at[step],
            device_id={"img": owner_at(step)},
            device_id_type=MESH,
        )

    def sent_copy(step):
        return pltpu.make_async_remote_copy(
            src_ref=sent.at[step],
            dst_ref=got.at[here],
            send_sem=sent_send.at[step],
            recv_sem=sent_recv.at[step],
            device_id={"head": head_at(step)},
            device_id_type=MESH,
        )

    each(owners - 1, lambda step: slot_copy(step + 1).start())
    for step in range(1, heads):
        merge_copy(step).start()

    for at in (0, 1, 2):
        local[at].wait()
    both = jnp.concatenate([value[...], shared[...]], axis=0)
    for img in range(per):
        pack[img] = lax.dot_general(
            desc[img], both, (((1,), (1,)), ((), ())), preferred_element_type=jnp.float32
        ).astype(jnp.bfloat16)

    def block_of(image):
        return lax.div(image + per, per) - 1

    def asked(owner):
        def body(slot, found):
            for side in range(2):
                image = all_slots[owner, 0, slot * 2 + side]
                found = jnp.where(block_of(image) == me, image - me * per, found)
            return found

        return fold(capacity, body, jnp.int32(-1))

    def send_pack(step):
        step = step + 1
        outgoing[step] = pack[jnp.maximum(asked(owner_at(step)), 0)]
        pack_copy(step).start()

    each(owners - 1, lambda step: slot_copy(step + 1).wait_recv())
    each(owners - 1, send_pack)
    incoming[me] = pack[jnp.maximum(asked(me), 0)]

    local[4].wait()
    own = desc[here]
    base[...] = jnp.dot(own, first[:width], preferred_element_type=jnp.float32)
    local[3].wait()
    for step in range(1, heads):
        merge_copy(step).wait_recv()
    lower = first[width:]
    for head in range(heads):
        mixed = jnp.dot(merge_all[head], lower, preferred_element_type=jnp.float32).astype(
            jnp.bfloat16
        )
        zero = jnp.zeros_like(mixed)
        at = head * 2 * HD
        merge_top[0, at : at + HD] = mixed
        merge_top[0, at + HD : at + 2 * HD] = zero
        merge_top[1, at : at + HD] = zero
        merge_top[1, at + HD : at + 2 * HD] = mixed

    each(owners - 1, lambda step: pack_copy(step + 1).wait_recv())
    lanes = lax.broadcasted_iota(jnp.int32, (points, 2 * HD), 1) < HD
    few = lax.broadcasted_iota(jnp.int32, (half, 2 * HD), 1) < HD
    column = lax.broadcasted_iota(jnp.int32, (half, points), 1)
    factor = math.log2(math.e) / math.sqrt(HD)

    def answer(step):
        block = owner_at(step)

        def body(slot, found):
            other, image = found
            one, two = slots[slot, 0], slots[slot, 1]
            block_one, block_two = block_of(one), block_of(two)
            is_one, is_two = block_one == block, block_two == block
            other = jnp.where(is_one, block_two, jnp.where(is_two, block_one, other))
            image = jnp.where(is_one, two, jnp.where(is_two, one, image))
            return other, image

        other, image = fold(capacity, body, (block, jnp.int32(0)))
        valid = column < counts[image]
        mine = incoming[block]
        theirs = incoming[other]
        keys = jnp.where(lanes, jnp.zeros_like(mine), mine)
        values = jnp.where(lanes, theirs, jnp.ones_like(theirs))
        parts = []
        for side in range(2):
            scores = lax.dot_general(
                keys[side * half : (side + 1) * half],
                theirs,
                (((1,), (1,)), ((), ())),
                preferred_element_type=jnp.float32,
            )
            scores = jnp.where(valid, scores, FAR)
            largest = jnp.max(scores, axis=1, keepdims=True)
            powers = jnp.exp2((scores - largest) * factor).astype(jnp.bfloat16)
            parts.append(jnp.dot(powers, values, preferred_element_type=jnp.float32))
        upper, under = parts
        top = jnp.where(few, upper, pltpu.roll(under, HD, 1))
        bottom = jnp.where(few, pltpu.roll(upper, HD, 1), under)
        return (top / bottom).astype(jnp.bfloat16)

    def reply(step):
        replies[step + 1] = answer(step + 1)
        reply_copy(step + 1).start()

    each(owners - 1, reply)
    returned[me] = answer(0)
    each(owners - 1, lambda step: reply_copy(step + 1).wait_recv())

    def message(image):
        def body(owner, total):
            hit = asked(owner) == image
            return total + jnp.where(hit, returned[owner].astype(jnp.float32), 0.0)

        return fold(owners, body, jnp.zeros((half, 2 * HD), jnp.float32)).astype(jnp.bfloat16)

    for step in range(1, heads):
        sent[step] = message(head_at(step))
        sent_copy(step).start()
    got[here] = message(here)
    for at in (5, 6, 7, 8):
        local[at].wait()
    for step in range(1, heads):
        sent_copy(step).wait_recv()

    rows = half // 2
    for side in range(2):
        for chunk in range(2):
            at = chunk * rows
            start = side * half + at
            joined = jnp.concatenate([got[head, at : at + rows] for head in range(heads)], axis=1)
            hidden = base[start : start + rows] + jnp.dot(
                joined, merge_top[side], preferred_element_type=jnp.float32
            )
            center = jnp.mean(hidden, axis=1, keepdims=True)
            moved = hidden - center
            spread = jnp.mean(jnp.square(moved), axis=1, keepdims=True)
            normed = moved * lax.rsqrt(spread + 1e-05) * gain[...] + bias[...]
            active = (normed * 0.5 * (1.0 + lax.erf(normed * math.sqrt(0.5)))).astype(jnp.bfloat16)
            update = jnp.dot(active, second[...], preferred_element_type=jnp.float32) + last[...]
            out[start : start + rows] = (
                desc[here, start : start + rows].astype(jnp.float32) + update
            ).astype(jnp.bfloat16)

    each(owners - 1, lambda step: slot_copy(step + 1).wait_send())
    each(owners - 1, lambda step: pack_copy(step + 1).wait_send())
    each(owners - 1, lambda step: reply_copy(step + 1).wait_send())
    for step in range(1, heads):
        merge_copy(step).wait_send()
        sent_copy(step).wait_send()


def on_device(owners, heads, *arrays):
    (
        descriptors,
        pair_slots,
        valid_counts,
        shared_proj,
        value_proj,
        merge_proj,
        first_layer,
        second_layer,
        norm_gain,
        norm_bias,
        second_bias,
    ) = arrays
    per, points, width = descriptors.shape
    half = points // 2
    inner = first_layer.shape[1]
    bf16 = jnp.bfloat16
    f32 = jnp.float32
    dma = pltpu.SemaphoreType.DMA
    smem = pl.BlockSpec(memory_space=pltpu.SMEM)
    anywhere = pl.BlockSpec(memory_space=pltpu.HBM)
    return pl.pallas_call(
        functools.partial(kernel, owners, heads),
        out_shape=jax.ShapeDtypeStruct((points, width), bf16),
        in_specs=[smem, smem] + [anywhere] * 9,
        out_specs=pl.BlockSpec(memory_space=pltpu.VMEM),
        scratch_shapes=[
            pltpu.VMEM(descriptors.shape, bf16),
            pltpu.VMEM(shared_proj.shape[::-1], bf16),
            pltpu.VMEM(value_proj.shape[::-1], bf16),
            pltpu.VMEM((heads,) + merge_proj.shape, bf16),
            pltpu.VMEM(first_layer.shape, bf16),
            pltpu.VMEM(second_layer.shape, bf16),
            pltpu.VMEM((1, inner), f32),
            pltpu.VMEM((1, inner), f32),
            pltpu.VMEM((1, width), f32),
            pltpu.SMEM((owners, 1, 2 * pair_slots.shape[0]), jnp.int32),
            pltpu.VMEM((per, points, 2 * HD), bf16),
            pltpu.VMEM((owners, points, 2 * HD), bf16),
            pltpu.VMEM((owners, points, 2 * HD), bf16),
            pltpu.VMEM((owners, half, 2 * HD), bf16),
            pltpu.VMEM((owners, half, 2 * HD), bf16),
            pltpu.VMEM((heads, half, 2 * HD), bf16),
            pltpu.VMEM((heads, half, 2 * HD), bf16),
            pltpu.VMEM((points, inner), f32),
            pltpu.VMEM((2, heads * 2 * HD, inner), bf16),
            dma((9,)),
            dma((owners,)),
            dma((owners,)),
            dma((heads,)),
            dma((heads,)),
            dma((owners,)),
            dma((owners,)),
            dma((owners,)),
            dma((owners,)),
            dma((heads,)),
            dma((heads,)),
        ],
        compiler_params=pltpu.CompilerParams(
            collective_id=0, has_side_effects=True, vmem_limit_bytes=48 * 2**20
        ),
    )(
        pair_slots,
        valid_counts,
        descriptors,
        shared_proj.T,
        value_proj.T,
        merge_proj,
        first_layer,
        second_layer,
        norm_gain.reshape(1, inner),
        norm_bias.reshape(1, inner),
        second_bias.reshape(1, width),
    )


def solution(mesh):
    return jax.shard_map(
        functools.partial(on_device, mesh.shape["img"], mesh.shape["head"]),
        mesh=mesh,
        in_specs=(
            P(("groups", "img"), None, None),
            P(("groups", "img"), None),
            P("groups"),
            P(None, "head"),
            P(None, "head"),
            P("head", None),
            P(),
            P(),
            P(),
            P(),
            P(),
        ),
        out_specs=P(("groups", "img", "head"), None),
        check_vma=False,
    )
```

time: 103 us -> 38.3 us (0.37)
  waiting for transfers between devices: 36.8 us -> 0 us
  Pallas kernels: 0 us -> 31 us
  blocking collectives: 22.3 us -> 0 us
  between operations: 13.6 us -> 0.02 us
  matrix products: 11.8 us -> 0 us
  other arithmetic: 4.53 us -> 0 us
  starting transfers between devices: 3.5 us -> 0 us
  loops' own time: 2.71 us -> 0 us
    pallas_call x0 -> x1, Pallas kernels: none -> 31 us  [on_device(): pl.pallas_call(functools.partial(kernel, owners, heads), out_shape=jax.Sh...]
    reduce_scatter x1 -> x0, waiting for transfers between devices: 27.1 us -> none  [on_device(): lax.psum_scatter(jnp.dot(message_rows, merge_proj, preferred_element_type...]
    all_gather x1 -> x0, blocking collectives: 13 us -> none  [on_device(): all_slots = lax.all_gather(pair_slots, 'img', axis=0, tiled=True)]
    dot_general x13 -> x0, matrix products: 11.8 us -> none  [the longest x1 2.77 us: on_device(): jnp.dot(active, second_layer, preferred_element_type=jnp.float32)]
    all_to_all x1 -> x0, waiting for transfers between devices: 9.66 us -> none  [on_device(): lax.all_to_all(outgoing, 'img', split_axis=0, concat_axis=0, tiled=True)]
    all_to_all x1 -> x0, blocking collectives: 9.32 us -> none  [on_device(): lax.all_to_all(replies, 'img', split_axis=0, concat_axis=0, tiled=True)]
    unnamed x21 -> x23, local copies, waits for them, and re-layouts: 0.24 us -> 6.8 us
    dynamic_slice x9 -> x0, local copies, waits for them, and re-layouts: 5.23 us -> none  [the longest x2 1.34 us: one_pair(): valid_counts[second_img]]
  transfers between devices with their start and end apart: 2 -> 0, of which waited for: 2 -> 0; matrix products, arithmetic and copies ran while one was open for 0% -> 0% of each run, Pallas kernels for 0% -> 0%
where the time goes in v1:
time: 38.3 us; the launch traced here: 37.8 us
  Pallas kernels  31 us (81%)
  local copies, waits for them, and re-layouts  6.8 us (18%)
    pallas_call x1, Pallas kernels, on_device(): pl.pallas_call(functools.partial(kernel, owners, heads), out_shape=jax.Sh...  31 us
    unnamed x23, local copies, waits for them, and re-layouts  6.8 us

profile of v1, /device:TPU:0, one launch (start us, length us, event | category | flops | bytes accessed | tf_op | source)
XLA Modules:
  0.0 37.8 jit_solution(15328638517145483477)
XLA Ops:
  0.0 0.0 copy-start.9
  0.0 0.0 copy-start.7
  0.0 0.0 copy-start.6
  0.0 0.0 copy-start.8
  0.0 0.0 copy-start.10
  0.0 0.7 %copy-done.9 = f32[256]{0:T(256)S(1)} copy-done((f32[256]{0:T(256)S(1)}, f32[256]{0:T(256)}, u32[]{:S(2)}) %copy-start.9) | copy-done | bytes 1048
  0.7 0.0 copy-done.7
  0.7 0.0 copy-done.6
  0.7 0.0 copy-done.8
  0.7 0.0 copy-done.10
  0.7 0.0 copy-start
  0.7 1.1 %copy-done = bf16[4,384,256]{2,1,0:T(8,128)(2,1)S(1)} copy-done((bf16[4,384,256]{2,1,0:T(8,128)(2,1)S(1)}, bf16[4,384,256]{2,1,0:T(8,128)(2,1)}, u32[]{:S(2)}) %copy-start) | copy-done | bytes 786456
  1.9 0.0 copy-start.1
  1.9 1.0 %copy-done.1 = bf16[512,512]{1,0:T(8,128)(2,1)S(1)} copy-done((bf16[512,512]{1,0:T(8,128)(2,1)S(1)}, bf16[512,512]{1,0:T(8,128)(2,1)}, u32[]{:S(2)}) %copy-start.1) | copy-done | bytes 524312
  2.9 0.0 copy-start.2
  2.9 0.9 %copy-done.2 = bf16[512,256]{1,0:T(8,128)(2,1)S(1)} copy-done((bf16[512,256]{1,0:T(8,128)(2,1)S(1)}, bf16[512,256]{1,0:T(8,128)(2,1)}, u32[]{:S(2)}) %copy-start.2) | copy-done | bytes 262168
  3.9 0.0 copy-start.3
  3.9 0.8 %copy-done.3 = bf16[256,64]{0,1:T(8,128)(2,1)S(1)} copy-done((bf16[256,64]{0,1:T(8,128)(2,1)S(1)}, bf16[256,64]{0,1:T(8,128)(2,1)}, u32[]{:S(2)}) %copy-start.3) | copy-done | bytes 32792
  4.6 0.0 copy-start.4
  4.6 0.8 %copy-done.4 = bf16[256,64]{0,1:T(8,128)(2,1)S(1)} copy-done((bf16[256,64]{0,1:T(8,128)(2,1)S(1)}, bf16[256,64]{0,1:T(8,128)(2,1)}, u32[]{:S(2)}) %copy-start.4) | copy-done | bytes 32792
  5.4 0.0 copy-start.5
  5.4 0.8 %copy-done.5 = bf16[64,256]{1,0:T(8,128)(2,1)S(1)} copy-done((bf16[64,256]{1,0:T(8,128)(2,1)S(1)}, bf16[64,256]{1,0:T(8,128)(2,1)}, u32[]{:S(2)}) %copy-start.5) | copy-done | bytes 32792
  6.1 31.0 %shard_map.109 = bf16[384,256]{1,0:T(8,128)(2,1)S(1)} custom-call(s32[2,2]{1,0:T(2,128)S(1)} %copy-done.8, s32[16]{0:T(128)S(1)} %copy-done.10, bf16[4,384,256]{2,1,0:T(8,128)(2,1)S(1)} %copy-done, bf16[64,256]{1,0:T(8,128)(2,1)S(1)} %bitcast.5, bf16[64,256]{1,0:T(8,128)(2,1)S(1)} %bitcast.6, bf16[64,256]{1,0:T(8,128)(2,1)S(1)} %copy-done.5, ...), custom_call_target="tpu_custom_call" | custom-call | tf_op jit(solution)/shard_map/pallas_call | solution.py:341
  37.1 0.7 %copy.13 = bf16[384,256]{1,0:T(8,128)(2,1)} copy(bf16[384,256]{1,0:T(8,128)(2,1)S(1)} %shard_map.109) | data formatting | bytes 393216
Async XLA Ops:
  0.0 0.7 %copy-start.9 = (f32[256]{0:T(256)S(1)}, f32[256]{0:T(256)}, u32[]{:S(2)}) copy-start(f32[256]{0:T(256)} %param.21) | copy-start | bytes 3076
  0.0 0.7 %copy-start.7 = (f32[512]{0:T(512)S(1)}, f32[512]{0:T(512)}, u32[]{:S(2)}) copy-start(f32[512]{0:T(512)} %param.20) | copy-start | bytes 6148
  0.0 0.7 %copy-start.6 = (f32[512]{0:T(512)S(1)}, f32[512]{0:T(512)}, u32[]{:S(2)}) copy-start(f32[512]{0:T(512)} %param.19) | copy-start | bytes 6148
  0.0 0.7 %copy-start.8 = (s32[2,2]{1,0:T(2,128)S(1)}, s32[2,2]{1,0:T(2,128)}, u32[]{:S(2)}) copy-start(s32[2,2]{1,0:T(2,128)} %slots.1) | copy-start | bytes 52
  0.0 0.7 %copy-start.10 = (s32[16]{0:T(128)S(1)}, s32[16]{0:T(128)}, u32[]{:S(2)}) copy-start(s32[16]{0:T(128)} %counts.1) | copy-start | bytes 196
  0.7 1.1 %copy-start = (bf16[4,384,256]{2,1,0:T(8,128)(2,1)S(1)}, bf16[4,384,256]{2,1,0:T(8,128)(2,1)}, u32[]{:S(2)}) copy-start(bf16[4,384,256]{2,1,0:T(8,128)(2,1)} %desc_in.1) | copy-start | bytes 2359300
  1.9 1.0 %copy-start.1 = (bf16[512,512]{1,0:T(8,128)(2,1)S(1)}, bf16[512,512]{1,0:T(8,128)(2,1)}, u32[]{:S(2)}) copy-start(bf16[512,512]{1,0:T(8,128)(2,1)} %first_in.1) | copy-start | bytes 1572868
  2.9 0.9 %copy-start.2 = (bf16[512,256]{1,0:T(8,128)(2,1)S(1)}, bf16[512,256]{1,0:T(8,128)(2,1)}, u32[]{:S(2)}) copy-start(bf16[512,256]{1,0:T(8,128)(2,1)} %second_in.1) | copy-start | bytes 786436
  3.9 0.8 %copy-start.3 = (bf16[256,64]{0,1:T(8,128)(2,1)S(1)}, bf16[256,64]{0,1:T(8,128)(2,1)}, u32[]{:S(2)}) copy-start(bf16[256,64]{0,1:T(8,128)(2,1)} %param.14) | copy-start | bytes 98308
  4.6 0.8 %copy-start.4 = (bf16[256,64]{0,1:T(8,128)(2,1)S(1)}, bf16[256,64]{0,1:T(8,128)(2,1)}, u32[]{:S(2)}) copy-start(bf16[256,64]{0,1:T(8,128)(2,1)} %param.15) | copy-start | bytes 98308
  5.4 0.8 %copy-start.5 = (bf16[64,256]{1,0:T(8,128)(2,1)S(1)}, bf16[64,256]{1,0:T(8,128)(2,1)}, u32[]{:S(2)}) copy-start(bf16[64,256]{1,0:T(8,128)(2,1)} %merge_in.1) | copy-start | bytes 98308

commit v2 on v1

--- a/solution.py
+++ b/solution.py
@@ -32,8 +32,8 @@
 def kernel(
     owners,
     heads,
-    slots,
-    counts,
+    slots_in,
+    counts_in,
     desc_in,
     shared_in,
     value_in,
@@ -43,7 +43,7 @@
     gain_in,
     bias_in,
     last_in,
-    out,
+    out_hbm,
     desc,
     shared,
     value,
@@ -53,6 +53,8 @@
     gain,
     bias,
     last,
+    slots,
+    counts,
     all_slots,
     pack,
     outgoing,
@@ -63,6 +65,8 @@
     got,
     base,
     merge_top,
+    out,
+    out_sem,
     local_sem,
     slot_send,
     slot_recv,
@@ -82,12 +86,39 @@
     here = lax.axis_index("head")
 
     def owner_at(shift):
-        return lax.rem(me + shift, owners)
+        if owners & (owners - 1):
+            return lax.rem(me + shift, owners)
+        bit, total = 1, 0
+        while bit < owners:
+            total += bit * lax.rem(lax.div(me, bit) + shift // bit, 2)
+            bit *= 2
+        return total
+
+    def each_peer(body):
+        order = [step for step in range(owners // 2, owners)] + list(range(1, owners // 2))
+        if owners <= 8:
+            for step in order:
+                body(step)
+        else:
+            lax.fori_loop(1, owners, lambda step, carry: (body(step), carry)[1], 0)
 
     def head_at(shift):
         return lax.rem(here + shift, heads)
 
+    barrier = pltpu.get_barrier_semaphore()
+    each_peer(
+        lambda step: pl.semaphore_signal(
+            barrier, inc=1, device_id={"img": owner_at(step)}, device_id_type=MESH
+        )
+    )
+    for step in range(1, heads):
+        pl.semaphore_signal(
+            barrier, inc=1, device_id={"head": head_at(step)}, device_id_type=MESH
+        )
+    direct = len(all_slots.shape) == 3 and all_slots.shape[1:] == slots_in.shape
     pairs = [
+        (slots_in, all_slots.at[me] if direct else slots),
+        (counts_in, counts),
         (desc_in, desc),
         (shared_in, shared),
         (value_in, value),
@@ -108,24 +139,20 @@
         all_slots[me, 0, slot * 2] = slots[slot, 0]
         all_slots[me, 0, slot * 2 + 1] = slots[slot, 1]
 
-    each(capacity, keep_slots)
-
-    barrier = pltpu.get_barrier_semaphore()
-    each(
-        owners - 1,
-        lambda step: pl.semaphore_signal(
-            barrier, inc=1, device_id={"img": owner_at(step + 1)}, device_id_type=MESH
-        ),
-    )
-    for step in range(1, heads):
-        pl.semaphore_signal(
-            barrier, inc=1, device_id={"head": head_at(step)}, device_id_type=MESH
-        )
+    def slot_at(owner, slot, side):
+        if direct:
+            return all_slots[owner, slot, side]
+        return all_slots[owner, 0, slot * 2 + side]
+
+    if not direct:
+        local[0].wait()
+        each(capacity, keep_slots)
+
     pl.semaphore_wait(barrier, owners + heads - 2)
 
     def slot_copy(step):
         return pltpu.make_async_remote_copy(
-            src_ref=all_slots.at[me],
+            src_ref=slots_in if direct else all_slots.at[me],
             dst_ref=all_slots.at[me],
             send_sem=slot_send.at[step],
             recv_sem=slot_recv.at[step],
@@ -173,11 +200,11 @@
             device_id_type=MESH,
         )
 
-    each(owners - 1, lambda step: slot_copy(step + 1).start())
+    each_peer(lambda step: slot_copy(step).start())
     for step in range(1, heads):
         merge_copy(step).start()
 
-    for at in (0, 1, 2):
+    for at in (2, 3, 4):
         local[at].wait()
     both = jnp.concatenate([value[...], shared[...]], axis=0)
     for img in range(per):
@@ -191,25 +218,26 @@
     def asked(owner):
         def body(slot, found):
             for side in range(2):
-                image = all_slots[owner, 0, slot * 2 + side]
+                image = slot_at(owner, slot, side)
                 found = jnp.where(block_of(image) == me, image - me * per, found)
             return found
 
         return fold(capacity, body, jnp.int32(-1))
 
     def send_pack(step):
-        step = step + 1
         outgoing[step] = pack[jnp.maximum(asked(owner_at(step)), 0)]
         pack_copy(step).start()
 
-    each(owners - 1, lambda step: slot_copy(step + 1).wait_recv())
-    each(owners - 1, send_pack)
+    if direct:
+        local[0].wait()
+    each_peer(lambda step: slot_copy(step).wait_recv())
+    each_peer(send_pack)
     incoming[me] = pack[jnp.maximum(asked(me), 0)]
 
-    local[4].wait()
+    local[6].wait()
     own = desc[here]
     base[...] = jnp.dot(own, first[:width], preferred_element_type=jnp.float32)
-    local[3].wait()
+    local[5].wait()
     for step in range(1, heads):
         merge_copy(step).wait_recv()
     lower = first[width:]
@@ -224,7 +252,8 @@
         merge_top[1, at : at + HD] = zero
         merge_top[1, at + HD : at + 2 * HD] = mixed
 
-    each(owners - 1, lambda step: pack_copy(step + 1).wait_recv())
+    each_peer(lambda step: pack_copy(step).wait_recv())
+    local[1].wait()
     lanes = lax.broadcasted_iota(jnp.int32, (points, 2 * HD), 1) < HD
     few = lax.broadcasted_iota(jnp.int32, (half, 2 * HD), 1) < HD
     column = lax.broadcasted_iota(jnp.int32, (half, points), 1)
@@ -235,7 +264,7 @@
 
         def body(slot, found):
             other, image = found
-            one, two = slots[slot, 0], slots[slot, 1]
+            one, two = slot_at(me, slot, 0), slot_at(me, slot, 1)
             block_one, block_two = block_of(one), block_of(two)
             is_one, is_two = block_one == block, block_two == block
             other = jnp.where(is_one, block_two, jnp.where(is_two, block_one, other))
@@ -266,12 +295,12 @@
         return (top / bottom).astype(jnp.bfloat16)
 
     def reply(step):
-        replies[step + 1] = answer(step + 1)
-        reply_copy(step + 1).start()
-
-    each(owners - 1, reply)
+        replies[step] = answer(step)
+        reply_copy(step).start()
+
+    each_peer(reply)
     returned[me] = answer(0)
-    each(owners - 1, lambda step: reply_copy(step + 1).wait_recv())
+    each_peer(lambda step: reply_copy(step).wait_recv())
 
     def message(image):
         def body(owner, total):
@@ -284,12 +313,17 @@
         sent[step] = message(head_at(step))
         sent_copy(step).start()
     got[here] = message(here)
-    for at in (5, 6, 7, 8):
+    for at in (7, 8, 9, 10):
         local[at].wait()
     for step in range(1, heads):
         sent_copy(step).wait_recv()
 
     rows = half // 2
+
+    def out_copy(chunk):
+        span = pl.ds(chunk * rows, rows)
+        return pltpu.make_async_copy(out.at[span], out_hbm.at[span], out_sem.at[chunk])
+
     for side in range(2):
         for chunk in range(2):
             at = chunk * rows
@@ -307,13 +341,15 @@
             out[start : start + rows] = (
                 desc[here, start : start + rows].astype(jnp.float32) + update
             ).astype(jnp.bfloat16)
-
-    each(owners - 1, lambda step: slot_copy(step + 1).wait_send())
-    each(owners - 1, lambda step: pack_copy(step + 1).wait_send())
-    each(owners - 1, lambda step: reply_copy(step + 1).wait_send())
+            out_copy(side * 2 + chunk).start()
+
+    each_peer(lambda step: slot_copy(step).wait_send())
+    each_peer(lambda step: pack_copy(step).wait_send())
+    each_peer(lambda step: reply_copy(step).wait_send())
     for step in range(1, heads):
         merge_copy(step).wait_send()
         sent_copy(step).wait_send()
+    each(4, lambda chunk: out_copy(chunk).wait())
 
 
 def on_device(owners, heads, *arrays):
@@ -333,16 +369,18 @@
     per, points, width = descriptors.shape
     half = points // 2
     inner = first_layer.shape[1]
+    capacity = pair_slots.shape[0]
+    small = owners * capacity <= 512
+    table = (owners, capacity, 2) if small else (owners, 1, 2 * capacity)
     bf16 = jnp.bfloat16
     f32 = jnp.float32
     dma = pltpu.SemaphoreType.DMA
-    smem = pl.BlockSpec(memory_space=pltpu.SMEM)
     anywhere = pl.BlockSpec(memory_space=pltpu.HBM)
     return pl.pallas_call(
         functools.partial(kernel, owners, heads),
         out_shape=jax.ShapeDtypeStruct((points, width), bf16),
-        in_specs=[smem, smem] + [anywhere] * 9,
-        out_specs=pl.BlockSpec(memory_space=pltpu.VMEM),
+        in_specs=[anywhere] * 11,
+        out_specs=anywhere,
         scratch_shapes=[
             pltpu.VMEM(descriptors.shape, bf16),
             pltpu.VMEM(shared_proj.shape[::-1], bf16),
@@ -353,7 +391,9 @@
             pltpu.VMEM((1, inner), f32),
             pltpu.VMEM((1, inner), f32),
             pltpu.VMEM((1, width), f32),
-            pltpu.SMEM((owners, 1, 2 * pair_slots.shape[0]), jnp.int32),
+            pltpu.SMEM(pair_slots.shape, jnp.int32),
+            pltpu.SMEM(valid_counts.shape, jnp.int32),
+            pltpu.SMEM(table, jnp.int32),
             pltpu.VMEM((per, points, 2 * HD), bf16),
             pltpu.VMEM((owners, points, 2 * HD), bf16),
             pltpu.VMEM((owners, points, 2 * HD), bf16),
@@ -363,7 +403,9 @@
             pltpu.VMEM((heads, half, 2 * HD), bf16),
             pltpu.VMEM((points, inner), f32),
             pltpu.VMEM((2, heads * 2 * HD, inner), bf16),
-            dma((9,)),
+            pltpu.VMEM((points, width), bf16),
+            dma((4,)),
+            dma((11,)),
             dma((owners,)),
             dma((owners,)),
             dma((heads,)),
@@ -376,7 +418,7 @@
             dma((heads,)),
         ],
         compiler_params=pltpu.CompilerParams(
-            collective_id=0, has_side_effects=True, vmem_limit_bytes=48 * 2**20
+            collective_id=0, has_side_effects=True, vmem_limit_bytes=56 * 2**20
         ),
     )(
         pair_slots,

time: 38.3 us -> 31.7 us (0.83)
  local copies, waits for them, and re-layouts: 6.8 us -> 1.62 us
  Pallas kernels: 31 us -> 29.9 us
    unnamed x23 -> x1, local copies, waits for them, and re-layouts: 6.8 us -> 1.62 us
    pallas_call x1, Pallas kernels: 31 us -> 29.9 us  [on_device(): pl.pallas_call(functools.partial(kernel, owners, heads), out_shape=jax.Sh...]
where the time goes in v2:
time: 31.7 us; the launch traced here: 31.5 us
  Pallas kernels  29.9 us (94%)
  local copies, waits for them, and re-layouts  1.62 us (5%)
    pallas_call x1, Pallas kernels, on_device(): pl.pallas_call(functools.partial(kernel, owners, heads), out_shape=jax.Sh...  29.9 us
    unnamed x1, local copies, waits for them, and re-layouts  1.62 us

profile of v2, /device:TPU:0, one launch (start us, length us, event | category | flops | bytes accessed | tf_op | source)
XLA Modules:
  0.0 31.5 jit_solution(11660377427423497536)
XLA Ops:
  0.0 29.9 %shard_map.109 = bf16[384,256]{1,0:T(8,128)(2,1)} custom-call(s32[2,2]{1,0:T(2,128)} %slots_in.1, s32[16]{0:T(128)} %counts_in.1, bf16[4,384,256]{2,1,0:T(8,128)(2,1)} %desc_in.1, bf16[64,256]{1,0:T(8,128)(2,1)} %bitcast.5, bf16[64,256]{1,0:T(8,128)(2,1)} %bitcast.6, bf16[64,256]{1,0:T(8,128)(2,1)} %merge_in.1, bf16[512,512]{1,0:T(8,128)(2,1)} %first_in.1, ...), custom_call_target="tpu_custom_call" | custom-call | tf_op jit(solution)/shard_map/pallas_call | solution.py:379
  29.9 1.6 %copy.13 = bf16[384,256]{1,0:T(8,128)(2,1)} copy(bf16[384,256]{1,0:T(8,128)(2,1)} %shard_map.109) | data formatting | bytes 393216

commit v3 on v2

--- a/solution.py
+++ b/solution.py
@@ -224,15 +224,23 @@
 
         return fold(capacity, body, jnp.int32(-1))
 
+    known = {}
+
+    def wanted(step):
+        return known[step] if owners <= 8 else asked(owner_at(step))
+
     def send_pack(step):
-        outgoing[step] = pack[jnp.maximum(asked(owner_at(step)), 0)]
+        slot_copy(step).wait_recv()
+        if owners <= 8:
+            known[step] = asked(owner_at(step))
+        outgoing[step] = pack[jnp.maximum(wanted(step), 0)]
         pack_copy(step).start()
 
+    each_peer(send_pack)
     if direct:
         local[0].wait()
-    each_peer(lambda step: slot_copy(step).wait_recv())
-    each_peer(send_pack)
-    incoming[me] = pack[jnp.maximum(asked(me), 0)]
+    known[0] = asked(me)
+    incoming[me] = pack[jnp.maximum(known[0], 0)]
 
     local[6].wait()
     own = desc[here]
@@ -252,14 +260,12 @@
         merge_top[1, at : at + HD] = zero
         merge_top[1, at + HD : at + 2 * HD] = mixed
 
-    each_peer(lambda step: pack_copy(step).wait_recv())
-    local[1].wait()
     lanes = lax.broadcasted_iota(jnp.int32, (points, 2 * HD), 1) < HD
     few = lax.broadcasted_iota(jnp.int32, (half, 2 * HD), 1) < HD
     column = lax.broadcasted_iota(jnp.int32, (half, points), 1)
     factor = math.log2(math.e) / math.sqrt(HD)
 
-    def answer(step):
+    def partner(step):
         block = owner_at(step)
 
         def body(slot, found):
@@ -272,7 +278,16 @@
             return other, image
 
         other, image = fold(capacity, body, (block, jnp.int32(0)))
-        valid = column < counts[image]
+        return block, other, counts[image]
+
+    local[1].wait()
+    if owners <= 8:
+        partners = [partner(step) for step in range(owners)]
+    each_peer(lambda step: pack_copy(step).wait_recv())
+
+    def answer(step):
+        block, other, count = partners[step] if owners <= 8 else partner(step)
+        valid = column < count
         mine = incoming[block]
         theirs = incoming[other]
         keys = jnp.where(lanes, jnp.zeros_like(mine), mine)
@@ -304,8 +319,9 @@
 
     def message(image):
         def body(owner, total):
-            hit = asked(owner) == image
-            return total + jnp.where(hit, returned[owner].astype(jnp.float32), 0.0)
+            hit = wanted(owner) == image
+            block = returned[owner_at(owner)]
+            return total + jnp.where(hit, block.astype(jnp.float32), 0.0)
 
         return fold(owners, body, jnp.zeros((half, 2 * HD), jnp.float32)).astype(jnp.bfloat16)
 

time: 31.7 us -> 30.8 us (0.972)
  Pallas kernels: 29.9 us -> 29 us
    pallas_call x1, Pallas kernels: 29.9 us -> 29 us  [on_device(): pl.pallas_call(functools.partial(kernel, owners, heads), out_shape=jax.Sh...]
where the time goes in v3:
time: 30.8 us; the launch traced here: 30.7 us
  Pallas kernels  29 us (94%)
  local copies, waits for them, and re-layouts  1.62 us (5%)
    pallas_call x1, Pallas kernels, on_device(): pl.pallas_call(functools.partial(kernel, owners, heads), out_shape=jax.Sh...  29 us
    unnamed x1, local copies, waits for them, and re-layouts  1.62 us

profile of v3, /device:TPU:0, one launch (start us, length us, event | category | flops | bytes accessed | tf_op | source)
XLA Modules:
  0.0 30.7 jit_solution(6401456281179621584)
XLA Ops:
  0.0 29.0 %shard_map.109 = bf16[384,256]{1,0:T(8,128)(2,1)} custom-call(s32[2,2]{1,0:T(2,128)} %slots_in.1, s32[16]{0:T(128)} %counts_in.1, bf16[4,384,256]{2,1,0:T(8,128)(2,1)} %desc_in.1, bf16[64,256]{1,0:T(8,128)(2,1)} %bitcast.5, bf16[64,256]{1,0:T(8,128)(2,1)} %bitcast.6, bf16[64,256]{1,0:T(8,128)(2,1)} %merge_in.1, bf16[512,512]{1,0:T(8,128)(2,1)} %first_in.1, ...), custom_call_target="tpu_custom_call" | custom-call | tf_op jit(solution)/shard_map/pallas_call | solution.py:395
  29.0 1.6 %copy.13 = bf16[384,256]{1,0:T(8,128)(2,1)} copy(bf16[384,256]{1,0:T(8,128)(2,1)} %shard_map.109) | data formatting | bytes 393216

commit v4 on v3

--- a/solution.py
+++ b/solution.py
@@ -95,7 +95,7 @@
         return total
 
     def each_peer(body):
-        order = [step for step in range(owners // 2, owners)] + list(range(1, owners // 2))
+        order = list(range(owners - 1, 0, -1))
         if owners <= 8:
             for step in order:
                 body(step)
@@ -334,14 +334,14 @@
     for step in range(1, heads):
         sent_copy(step).wait_recv()
 
-    rows = half // 2
+    rows = half
 
     def out_copy(chunk):
         span = pl.ds(chunk * rows, rows)
         return pltpu.make_async_copy(out.at[span], out_hbm.at[span], out_sem.at[chunk])
 
     for side in range(2):
-        for chunk in range(2):
+        for chunk in range(1):
             at = chunk * rows
             start = side * half + at
             joined = jnp.concatenate([got[head, at : at + rows] for head in range(heads)], axis=1)
@@ -357,7 +357,7 @@
             out[start : start + rows] = (
                 desc[here, start : start + rows].astype(jnp.float32) + update
             ).astype(jnp.bfloat16)
-            out_copy(side * 2 + chunk).start()
+            out_copy(side).start()
 
     each_peer(lambda step: slot_copy(step).wait_send())
     each_peer(lambda step: pack_copy(step).wait_send())
@@ -365,7 +365,7 @@
     for step in range(1, heads):
         merge_copy(step).wait_send()
         sent_copy(step).wait_send()
-    each(4, lambda chunk: out_copy(chunk).wait())
+    each(2, lambda chunk: out_copy(chunk).wait())
 
 
 def on_device(owners, heads, *arrays):
@@ -420,7 +420,7 @@
             pltpu.VMEM((points, inner), f32),
             pltpu.VMEM((2, heads * 2 * HD, inner), bf16),
             pltpu.VMEM((points, width), bf16),
-            dma((4,)),
+            dma((2,)),
             dma((11,)),
             dma((owners,)),
             dma((owners,)),

time: 30.8 us -> 29.8 us (0.968)
  Pallas kernels: 29 us -> 28 us
    pallas_call x1, Pallas kernels: 29 us -> 28 us  [on_device(): pl.pallas_call(functools.partial(kernel, owners, heads), out_shape=jax.Sh...]
where the time goes in v4:
time: 29.8 us; the launch traced here: 29.7 us
  Pallas kernels  28 us (94%)
  local copies, waits for them, and re-layouts  1.62 us (5%)
    pallas_call x1, Pallas kernels, on_device(): pl.pallas_call(functools.partial(kernel, owners, heads), out_shape=jax.Sh...  28 us
    unnamed x1, local copies, waits for them, and re-layouts  1.62 us

profile of v4, /device:TPU:0, one launch (start us, length us, event | category | flops | bytes accessed | tf_op | source)
XLA Modules:
  0.0 29.7 jit_solution(5314617867715997744)
XLA Ops:
  0.0 28.0 %shard_map.109 = bf16[384,256]{1,0:T(8,128)(2,1)} custom-call(s32[2,2]{1,0:T(2,128)} %slots_in.1, s32[16]{0:T(128)} %counts_in.1, bf16[4,384,256]{2,1,0:T(8,128)(2,1)} %desc_in.1, bf16[64,256]{1,0:T(8,128)(2,1)} %bitcast.5, bf16[64,256]{1,0:T(8,128)(2,1)} %bitcast.6, bf16[64,256]{1,0:T(8,128)(2,1)} %merge_in.1, bf16[512,512]{1,0:T(8,128)(2,1)} %first_in.1, ...), custom_call_target="tpu_custom_call" | custom-call | tf_op jit(solution)/shard_map/pallas_call | solution.py:395
  28.1 1.6 %copy.13 = bf16[384,256]{1,0:T(8,128)(2,1)} copy(bf16[384,256]{1,0:T(8,128)(2,1)} %shard_map.109) | data formatting | bytes 393216
